TPU v7x, 256 devices: a whole 4x4x8 slice. The times are simulated.
256 devices in a mesh: segment: 16 (over x_lo, z), tp: 16 (over y, x_hi, core).
Axes of the slice: x: 4 (x_hi: 2, x_lo: 2; x = x_hi * 2 + x_lo), y: 4, z: 8, core: 2. Of those that a mesh axis runs over, the one named last changes fastest.
Arguments:
- layer_inputs: bfloat16 [16, 2, 128, 2048], P('segment', None, 'tp'), may hold values from -100 to 100, as said below
- cotangent: bfloat16 [2, 2, 128, 2048], P(None, None, 'tp'), may hold values from -6 to 6
- gate_weight: bfloat16 [16, 2048, 4096], P('segment', None, 'tp'), may hold values from -1 to 1, as said below
- up_weight: bfloat16 [16, 2048, 4096], P('segment', None, 'tp'), may hold values from -1 to 1, as said below
- down_weight: bfloat16 [16, 4096, 2048], P('segment', 'tp'), may hold values from -1 to 1, as said below
- gate_momentum: float32 [16, 1024, 4096], P('segment', None, 'tp'), may hold values from -48 to 48
- up_momentum: float32 [16, 1024, 4096], P('segment', None, 'tp'), may hold values from -48 to 48
- down_momentum: float32 [16, 4096, 1024], P('segment', 'tp'), may hold values from -48 to 48
Outputs:
- input_gradient: bfloat16 [16, 2, 128, 2048], P('segment', None, 'tp')
- new_gate_momentum: float32 [16, 1024, 4096], P('segment', None, 'tp')
- new_up_momentum: float32 [16, 1024, 4096], P('segment', None, 'tp')
- new_down_momentum: float32 [16, 4096, 1024], P('segment', 'tp')
Inputs may be any that keep to these rules, and one draw needn't show every extreme that they name: `layer_inputs`: stored layer inputs, independent for every section and micro-batch. `gate_weight`: sections 2l and 2l + 1 hold equal copies of one layer's weights. `up_weight`: sections 2l and 2l + 1 hold equal copies of one layer's weights. `down_weight`: sections 2l and 2l + 1 hold equal copies of one layer's weights.
All inputs are finite; a program needn't handle non-finite values.
Results may differ from a plain program's by a relative error of at most 0.02.
Values may be sent and summed in bfloat16 or wider, within the bound.
No kernel may reach another device: no remote copies, remote signals or barrier semaphores. Data moves between devices by JAX's collectives and lax.ppermute only.
A program may use at most 64 MiB of HBM per device.

v0:
```python
import jax
import jax.numpy as jnp
from jax import lax
from jax.sharding import PartitionSpec as P

epsilon = 1e-05
momentum_decay = 0.9


def passed_along(block, axis, distance):
    devices = range(lax.axis_size(axis))
    route = [(i - distance, i) for i in devices if i - distance in devices]
    return lax.ppermute(block, axis, route)


def partner(block, axis, distance):
    count = lax.axis_size(axis)
    route = []
    for low in range(count):
        high = low | 1 << distance
        if high != low and high < count:
            route += [(low, high), (high, low)]
    return lax.ppermute(block, axis, route)


def contract_last(left, right):
    return lax.dot_general(
        left, right, (((1,), (1,)), ((), ())), preferred_element_type=jnp.float32
    )


def contract_rows(left, right):
    return lax.dot_general(
        left, right, (((0,), (0,)), ((), ())), preferred_element_type=jnp.float32
    )


def project(rows, gate_w, up_w):
    gate = jnp.dot(rows, gate_w, preferred_element_type=jnp.float32)
    up = jnp.dot(rows, up_w, preferred_element_type=jnp.float32)
    return (gate, up)


def backward_factors(incoming_rows, gate, up, down_w):
    hidden_grad = contract_last(incoming_rows, down_w)
    sigma = jax.nn.sigmoid(gate)
    silu = gate * sigma
    hidden = (silu * up).astype(jnp.bfloat16)
    gate_grad = (hidden_grad * up * sigma * (1.0 + gate * (1.0 - sigma))).astype(jnp.bfloat16)
    up_grad = (hidden_grad * silu).astype(jnp.bfloat16)
    return (hidden, gate_grad, up_grad)


def owned(array, start, size, axis):
    return lax.dynamic_slice_in_dim(array, start, size, axis)


def shards(
    layer_inputs,
    cotangent,
    gate_weight,
    up_weight,
    down_weight,
    gate_momentum,
    up_momentum,
    down_momentum,
):
    segments = lax.axis_size("segment")
    depth = segments // 2
    segment = lax.axis_index("segment")
    direction = segment % 2
    lower = direction == 0
    position = segment // 2
    gate_w = gate_weight[0]
    up_w = up_weight[0]
    down_w = down_weight[0]
    inputs = layer_inputs[0].astype(jnp.float32)
    micro, rows_dev, width = inputs.shape
    half = width // 2
    hidden_dev = gate_w.shape[1]
    total_rows = rows_dev * lax.axis_size("tp")
    inverse_norm = lax.rsqrt(jnp.mean(inputs * inputs, axis=-1, keepdims=True) + epsilon)
    exact = inputs * inverse_norm
    normed = exact.astype(jnp.bfloat16)
    entry = lax.dynamic_index_in_dim(cotangent, direction, 0, keepdims=False)
    ticks = depth + micro - 1
    extra = (
        jnp.zeros((width, hidden_dev), jnp.float32),
        jnp.zeros((width, hidden_dev), jnp.float32),
        jnp.zeros((hidden_dev, width), jnp.float32),
    )

    def process(tick, received, state):
        outgoing, backs, extra = state
        index = tick - position
        active = (index >= 0) & (index < micro)
        slot = jnp.clip(index, 0, micro - 1)
        local_in = jnp.where(position == 0, entry[slot], received)
        incoming_rows = lax.all_gather(local_in, "tp", axis=0, tiled=True)
        full_rows = lax.all_gather(normed[slot], "tp", axis=0, tiled=True)

        def factors():
            gate, up = project(full_rows, gate_w, up_w)
            return backward_factors(incoming_rows, gate, up, down_w)

        def resting():
            blank = jnp.zeros((total_rows, hidden_dev), jnp.bfloat16)
            return (blank, blank, blank)

        hidden, gate_grad, up_grad = lax.cond(active, factors, resting)
        count = lax.axis_size("tp") * rows_dev

        def compute():
            return contract_last(gate_grad, gate_w) + contract_last(up_grad, up_w)

        def quiet():
            return jnp.zeros((count, width), jnp.float32)

        normed_grad = lax.psum_scatter(
            lax.cond(active, compute, quiet).astype(jnp.bfloat16),
            "tp",
            scatter_dimension=0,
            tiled=True,
        ).astype(jnp.float32)
        scale = inverse_norm[slot]
        base = exact[slot]
        back = local_in.astype(jnp.float32) + scale * (
            normed_grad - base * jnp.mean(normed_grad * base, axis=-1, keepdims=True)
        )
        back = back.astype(jnp.bfloat16)
        backs = lax.dynamic_update_index_in_dim(
            backs, jnp.where(active, back, backs[slot]), slot, 0
        )

        def accumulate(totals):
            return (
                totals[0] + contract_rows(full_rows, gate_grad),
                totals[1] + contract_rows(full_rows, up_grad),
                totals[2] + contract_rows(hidden, incoming_rows),
            )

        def unchanged(totals):
            return totals

        extra = lax.cond(active, accumulate, unchanged, extra)
        return (back, backs, extra)

    zero_rows = jnp.zeros((rows_dev, width), jnp.bfloat16)
    state = process(
        0, zero_rows, (zero_rows, jnp.zeros((micro, rows_dev, width), jnp.bfloat16), extra)
    )

    def advance(tick, state):
        received = passed_along(state[0], "segment", 2)
        return process(tick, received, state)

    outgoing, backs, extra = lax.fori_loop(1, ticks, advance, state)
    keep_start = jnp.where(lower, 0, half)
    send_start = half - keep_start
    gate_total, up_total, down_total = extra
    arrived = partner(
        (
            owned(gate_total, send_start, half, 0).astype(jnp.bfloat16),
            owned(up_total, send_start, half, 0).astype(jnp.bfloat16),
            owned(down_total, send_start, half, 1).astype(jnp.bfloat16),
        ),
        "segment",
        0,
    )
    gate_share = owned(gate_total, keep_start, half, 0) + arrived[0].astype(jnp.float32)
    up_share = owned(up_total, keep_start, half, 0) + arrived[1].astype(jnp.float32)
    down_share = owned(down_total, keep_start, half, 1) + arrived[2].astype(jnp.float32)
    new_gate = (momentum_decay * gate_momentum[0] + gate_share)[None]
    new_up = (momentum_decay * up_momentum[0] + up_share)[None]
    new_down = (momentum_decay * down_momentum[0] + down_share)[None]
    return (backs[None], new_gate, new_up, new_down)


def solution(mesh):
    return jax.shard_map(
        shards,
        mesh=mesh,
        in_specs=(
            P("segment", None, "tp", None),
            P(None, None, "tp", None),
            P("segment", None, "tp"),
            P("segment", None, "tp"),
            P("segment", "tp", None),
            P("segment", None, "tp"),
            P("segment", None, "tp"),
            P("segment", "tp", None),
        ),
        out_specs=(
            P("segment", None, "tp", None),
            P("segment", None, "tp"),
            P("segment", None, "tp"),
            P("segment", "tp", None),
        ),
        check_vma=False,
    )
```

profile of v0, /device:TPU:227, one launch (start us, length us, event | category | flops | bytes accessed | tf_op | source)
XLA Modules:
  0.0 1200.9 jit_solution(18428818250983817290)
XLA Ops:
  8.2 1.6 convert_multiply_fusion.1
  10.5 26.3 %all-gather.1 = bf16[1,128,2048]{2,1,0:T(8,128)(2,1)S(1)} all-gather(bf16[1,8,2048]{2,1,0:T(8,128)(2,1)S(1)} %constant_dynamic-slice_fusion.3), channel_id=3, replica_groups=mesh['segment'=16,'tp'=16] {'tp'}, dimensions={1}, use_global_device_ids=true | all-gather | bytes 557056 | tf_op jit(solution)/shard_map/all_gather | solution.py:100
  37.6 23.0 %all-gather.2 = bf16[1,1,128,2048]{3,2,1,0:T(8,128)(2,1)} all-gather(bf16[1,1,8,2048]{3,2,1,0:T(8,128)(2,1)S(1)} %dynamic-slice_select_fusion), channel_id=4, replica_groups=mesh['segment'=16,'tp'=16] {'tp'}, dimensions={2}, use_global_device_ids=true | all-gather | bytes 557056 | tf_op jit(solution)/shard_map/all_gather | solution.py:99
  61.6 4.5 conditional.8
  61.6 1.5 broadcast.81
  63.0 1.4 broadcast.81.clone
  64.5 1.6 broadcast_in_dim.27
  66.7 65.6 %reduce-scatter.3.cloned.1.call-done = bf16[8,2048]{1,0:T(8,128)(2,1)} async-done(((bf16[128,2048]{1,0:T(8,128)(2,1)}), bf16[8,2048]{1,0:T(8,128)(2,1)}) %reduce-scatter.3.cloned.1.call-update) | async-done | bytes 32784 | tf_op jit(solution)/shard_map/reduce_scatter | solution.py:119
  133.3 1.5 bitcast_dynamic-update-slice_fusion.1
  135.4 1021.5 %while.22 = (s32[]{:T(128)}, bf16[8,2048]{1,0:T(8,128)(2,1)}, bf16[2,8,2048]{2,1,0:T(8,128)(2,1)}, f32[2048,256]{1,0:T(8,128)}, f32[2048,256]{1,0:T(8,128)}, /*i...) while((s32[]{:T(128)}, bf16[8,2048]{1,0:T(8,128)(2,1)}, ...), condition=%wide.region_18.19_spmd, body=%wide.region_9.18_spmd.sunk | while | flops 1076527104 | bytes 32310056 | solution.py:157
  135.4 1.3 collective-permute-start
  137.5 26.4 %all-gather.4 = bf16[1,128,2048]{2,1,0:T(8,128)(2,1)S(1)} all-gather(bf16[1,8,2048]{2,1,0:T(8,128)(2,1)S(1)} %constant_dynamic-slice_fusion.8), channel_id=2, replica_groups=mesh['segment'=16,'tp'=16] {'tp'}, dimensions={1}, use_global_device_ids=true | all-gather | bytes 557056 | tf_op jit(solution)/shard_map/while/body/eval_jaxpr/all_gather | solution.py:100
  164.7 21.8 %all_gather.25 = bf16[128,2048]{1,0:T(8,128)(2,1)S(1)} all-gather(bf16[8,2048]{1,0:T(8,128)(2,1)S(1)} %bitcast_select_fusion.3), channel_id=1, replica_groups=mesh['segment'=16,'tp'=16] {'tp'}, dimensions={0}, use_global_device_ids=true | all-gather | bytes 557056 | tf_op jit(solution)/shard_map/while/body/eval_jaxpr/all_gather | solution.py:99
  188.2 72.6 %reduce-scatter.5.cloned.1.call-done = bf16[8,2048]{1,0:T(8,128)(2,1)} async-done(((bf16[128,2048]{1,0:T(8,128)(2,1)}), bf16[8,2048]{1,0:T(8,128)(2,1)}) %reduce-scatter.5.cloned.1.call-update) | async-done | bytes 32784 | tf_op jit(solution)/shard_map/while/body/eval_jaxpr/reduce_scatter | solution.py:119
  261.7 1.5 bitcast_dynamic-update-slice_fusion.3
  263.2 1.3 collective-permute-start
  265.3 26.4 %all-gather.4 = bf16[1,128,2048]{2,1,0:T(8,128)(2,1)S(1)} all-gather(bf16[1,8,2048]{2,1,0:T(8,128)(2,1)S(1)} %constant_dynamic-slice_fusion.8), channel_id=2, replica_groups=mesh['segment'=16,'tp'=16] {'tp'}, dimensions={1}, use_global_device_ids=true | all-gather | bytes 557056 | tf_op jit(solution)/shard_map/while/body/eval_jaxpr/all_gather | solution.py:100
  292.5 21.8 %all_gather.25 = bf16[128,2048]{1,0:T(8,128)(2,1)S(1)} all-gather(bf16[8,2048]{1,0:T(8,128)(2,1)S(1)} %bitcast_select_fusion.3), channel_id=1, replica_groups=mesh['segment'=16,'tp'=16] {'tp'}, dimensions={0}, use_global_device_ids=true | all-gather | bytes 557056 | tf_op jit(solution)/shard_map/while/body/eval_jaxpr/all_gather | solution.py:99
  316.0 72.7 %reduce-scatter.5.cloned.1.call-done = bf16[8,2048]{1,0:T(8,128)(2,1)} async-done(((bf16[128,2048]{1,0:T(8,128)(2,1)}), bf16[8,2048]{1,0:T(8,128)(2,1)}) %reduce-scatter.5.cloned.1.call-update) | async-done | bytes 32784 | tf_op jit(solution)/shard_map/while/body/eval_jaxpr/reduce_scatter | solution.py:119
  389.6 1.5 bitcast_dynamic-update-slice_fusion.3
  393.2 26.4 %all-gather.4 = bf16[1,128,2048]{2,1,0:T(8,128)(2,1)S(1)} all-gather(bf16[1,8,2048]{2,1,0:T(8,128)(2,1)S(1)} %constant_dynamic-slice_fusion.8), channel_id=2, replica_groups=mesh['segment'=16,'tp'=16] {'tp'}, dimensions={1}, use_global_device_ids=true | all-gather | bytes 557056 | tf_op jit(solution)/shard_map/while/body/eval_jaxpr/all_gather | solution.py:100
  420.4 21.8 %all_gather.25 = bf16[128,2048]{1,0:T(8,128)(2,1)S(1)} all-gather(bf16[8,2048]{1,0:T(8,128)(2,1)S(1)} %bitcast_select_fusion.3), channel_id=1, replica_groups=mesh['segment'=16,'tp'=16] {'tp'}, dimensions={0}, use_global_device_ids=true | all-gather | bytes 557056 | tf_op jit(solution)/shard_map/while/body/eval_jaxpr/all_gather | solution.py:99
  443.9 72.7 %reduce-scatter.5.cloned.1.call-done = bf16[8,2048]{1,0:T(8,128)(2,1)} async-done(((bf16[128,2048]{1,0:T(8,128)(2,1)}), bf16[8,2048]{1,0:T(8,128)(2,1)}) %reduce-scatter.5.cloned.1.call-update) | async-done | bytes 32784 | tf_op jit(solution)/shard_map/while/body/eval_jaxpr/reduce_scatter | solution.py:119
  517.5 1.5 bitcast_dynamic-update-slice_fusion.3
  521.1 26.4 %all-gather.4 = bf16[1,128,2048]{2,1,0:T(8,128)(2,1)S(1)} all-gather(bf16[1,8,2048]{2,1,0:T(8,128)(2,1)S(1)} %constant_dynamic-slice_fusion.8), channel_id=2, replica_groups=mesh['segment'=16,'tp'=16] {'tp'}, dimensions={1}, use_global_device_ids=true | all-gather | bytes 557056 | tf_op jit(solution)/shard_map/while/body/eval_jaxpr/all_gather | solution.py:100
  548.2 21.9 %all_gather.25 = bf16[128,2048]{1,0:T(8,128)(2,1)S(1)} all-gather(bf16[8,2048]{1,0:T(8,128)(2,1)S(1)} %bitcast_select_fusion.3), channel_id=1, replica_groups=mesh['segment'=16,'tp'=16] {'tp'}, dimensions={0}, use_global_device_ids=true | all-gather | bytes 557056 | tf_op jit(solution)/shard_map/while/body/eval_jaxpr/all_gather | solution.py:99
  571.8 71.9 %reduce-scatter.5.cloned.1.call-done = bf16[8,2048]{1,0:T(8,128)(2,1)} async-done(((bf16[128,2048]{1,0:T(8,128)(2,1)}), bf16[8,2048]{1,0:T(8,128)(2,1)}) %reduce-scatter.5.cloned.1.call-update) | async-done | bytes 32784 | tf_op jit(solution)/shard_map/while/body/eval_jaxpr/reduce_scatter | solution.py:119
  644.6 1.5 bitcast_dynamic-update-slice_fusion.3
  648.2 26.4 %all-gather.4 = bf16[1,128,2048]{2,1,0:T(8,128)(2,1)S(1)} all-gather(bf16[1,8,2048]{2,1,0:T(8,128)(2,1)S(1)} %constant_dynamic-slice_fusion.8), channel_id=2, replica_groups=mesh['segment'=16,'tp'=16] {'tp'}, dimensions={1}, use_global_device_ids=true | all-gather | bytes 557056 | tf_op jit(solution)/shard_map/while/body/eval_jaxpr/all_gather | solution.py:100
  675.4 21.8 %all_gather.25 = bf16[128,2048]{1,0:T(8,128)(2,1)S(1)} all-gather(bf16[8,2048]{1,0:T(8,128)(2,1)S(1)} %bitcast_select_fusion.3), channel_id=1, replica_groups=mesh['segment'=16,'tp'=16] {'tp'}, dimensions={0}, use_global_device_ids=true | all-gather | bytes 557056 | tf_op jit(solution)/shard_map/while/body/eval_jaxpr/all_gather | solution.py:99
  698.9 73.1 %reduce-scatter.5.cloned.1.call-done = bf16[8,2048]{1,0:T(8,128)(2,1)} async-done(((bf16[128,2048]{1,0:T(8,128)(2,1)}), bf16[8,2048]{1,0:T(8,128)(2,1)}) %reduce-scatter.5.cloned.1.call-update) | async-done | bytes 32784 | tf_op jit(solution)/shard_map/while/body/eval_jaxpr/reduce_scatter | solution.py:119
  772.9 1.5 bitcast_dynamic-update-slice_fusion.3
  776.5 26.4 %all-gather.4 = bf16[1,128,2048]{2,1,0:T(8,128)(2,1)S(1)} all-gather(bf16[1,8,2048]{2,1,0:T(8,128)(2,1)S(1)} %constant_dynamic-slice_fusion.8), channel_id=2, replica_groups=mesh['segment'=16,'tp'=16] {'tp'}, dimensions={1}, use_global_device_ids=true | all-gather | bytes 557056 | tf_op jit(solution)/shard_map/while/body/eval_jaxpr/all_gather | solution.py:100
  803.7 21.8 %all_gather.25 = bf16[128,2048]{1,0:T(8,128)(2,1)S(1)} all-gather(bf16[8,2048]{1,0:T(8,128)(2,1)S(1)} %bitcast_select_fusion.3), channel_id=1, replica_groups=mesh['segment'=16,'tp'=16] {'tp'}, dimensions={0}, use_global_device_ids=true | all-gather | bytes 557056 | tf_op jit(solution)/shard_map/while/body/eval_jaxpr/all_gather | solution.py:99
  827.2 73.2 %reduce-scatter.5.cloned.1.call-done = bf16[8,2048]{1,0:T(8,128)(2,1)} async-done(((bf16[128,2048]{1,0:T(8,128)(2,1)}), bf16[8,2048]{1,0:T(8,128)(2,1)}) %reduce-scatter.5.cloned.1.call-update) | async-done | bytes 32784 | tf_op jit(solution)/shard_map/while/body/eval_jaxpr/reduce_scatter | solution.py:119
  901.3 1.5 bitcast_dynamic-update-slice_fusion.3
  904.8 26.4 %all-gather.4 = bf16[1,128,2048]{2,1,0:T(8,128)(2,1)S(1)} all-gather(bf16[1,8,2048]{2,1,0:T(8,128)(2,1)S(1)} %constant_dynamic-slice_fusion.8), channel_id=2, replica_groups=mesh['segment'=16,'tp'=16] {'tp'}, dimensions={1}, use_global_device_ids=true | all-gather | bytes 557056 | tf_op jit(solution)/shard_map/while/body/eval_jaxpr/all_gather | solution.py:100
  932.0 21.8 %all_gather.25 = bf16[128,2048]{1,0:T(8,128)(2,1)S(1)} all-gather(bf16[8,2048]{1,0:T(8,128)(2,1)S(1)} %bitcast_select_fusion.3), channel_id=1, replica_groups=mesh['segment'=16,'tp'=16] {'tp'}, dimensions={0}, use_global_device_ids=true | all-gather | bytes 557056 | tf_op jit(solution)/shard_map/while/body/eval_jaxpr/all_gather | solution.py:99
  953.8 1.7 conditional.12
  955.6 1.8 conditional.13
  958.1 10.2 conditional.14
  958.1 3.4 convolution_add_fusion.4
  961.5 3.4 convolution_add_fusion.3
  964.9 3.4 convolution_add_fusion.2
  968.3 60.5 %reduce-scatter.5.cloned.1.call-done = bf16[8,2048]{1,0:T(8,128)(2,1)} async-done(((bf16[128,2048]{1,0:T(8,128)(2,1)}), bf16[8,2048]{1,0:T(8,128)(2,1)}) %reduce-scatter.5.cloned.1.call-update) | async-done | bytes 32784 | tf_op jit(solution)/shard_map/while/body/eval_jaxpr/reduce_scatter | solution.py:119
  1029.7 1.5 bitcast_dynamic-update-slice_fusion.3
  1033.2 26.4 %all-gather.4 = bf16[1,128,2048]{2,1,0:T(8,128)(2,1)S(1)} all-gather(bf16[1,8,2048]{2,1,0:T(8,128)(2,1)S(1)} %constant_dynamic-slice_fusion.8), channel_id=2, replica_groups=mesh['segment'=16,'tp'=16] {'tp'}, dimensions={1}, use_global_device_ids=true | all-gather | bytes 557056 | tf_op jit(solution)/shard_map/while/body/eval_jaxpr/all_gather | solution.py:100
  1060.4 21.8 %all_gather.25 = bf16[128,2048]{1,0:T(8,128)(2,1)S(1)} all-gather(bf16[8,2048]{1,0:T(8,128)(2,1)S(1)} %bitcast_select_fusion.3), channel_id=1, replica_groups=mesh['segment'=16,'tp'=16] {'tp'}, dimensions={0}, use_global_device_ids=true | all-gather | bytes 557056 | tf_op jit(solution)/shard_map/while/body/eval_jaxpr/all_gather | solution.py:99
  1082.3 1.7 conditional.12
  1084.0 1.8 conditional.13
  1086.6 10.2 conditional.14
  1086.6 3.4 convolution_add_fusion.4
  1090.0 3.4 convolution_add_fusion.3
  1093.3 3.4 convolution_add_fusion.2
  1096.7 57.8 %reduce-scatter.5.cloned.1.call-done = bf16[8,2048]{1,0:T(8,128)(2,1)} async-done(((bf16[128,2048]{1,0:T(8,128)(2,1)}), bf16[8,2048]{1,0:T(8,128)(2,1)}) %reduce-scatter.5.cloned.1.call-update) | async-done | bytes 32784 | tf_op jit(solution)/shard_map/while/body/eval_jaxpr/reduce_scatter | solution.py:119
  1155.4 1.5 bitcast_dynamic-update-slice_fusion.3
  1156.9 1.4 dynamic-slice_convert_fusion.2
  1161.2 1.3 dynamic-slice_convert_fusion
  1163.7 5.7 collective-permute-done.1
  1169.4 2.3 fusion.9
  1171.8 8.9 collective-permute-done.2
  1180.7 2.3 fusion.8
  1183.0 8.9 collective-permute-done.3
  1191.9 2.4 fusion.7
  (171 shorter events, 60.8 us)
Async XLA Ops:
  7.2 125.2 %reduce-scatter.3.cloned.1.call-start = ((), (), s32[]{:S(2)}) async-start(), calls=%async_computation.2 | async-start | bytes 557056 | tf_op jit(solution)/shard_map/reduce_scatter | solution.py:119
  60.7 0.8 copy-start.3
  61.5 4.6 copy-start.8
  61.5 73.8 %copy-start = (bf16[1,2048,256]{2,1,0:T(8,128)(2,1)S(1)}, bf16[1,2048,256]{2,1,0:T(8,128)(2,1)}, u32[]{:S(2)}) copy-start(bf16[1,2048,256]{2,1,0:T(8,128)(2,1)} %param.24) | copy-start | bytes 3145732
  61.5 73.8 %copy-start.1 = (bf16[1,2048,256]{2,1,0:T(8,128)(2,1)S(1)}, bf16[1,2048,256]{2,1,0:T(8,128)(2,1)}, u32[]{:S(2)}) copy-start(bf16[1,2048,256]{2,1,0:T(8,128)(2,1)} %param.25) | copy-start | bytes 3145732
  134.7 0.6 copy-start.7
  135.4 125.5 %reduce-scatter.5.cloned.1.call-start = ((), (), s32[]{:S(2)}) async-start(), calls=%async_computation.3 | async-start | bytes 557056 | tf_op jit(solution)/shard_map/while/body/eval_jaxpr/reduce_scatter | solution.py:119
  135.4 28.5 %collective-permute-start = (bf16[8,2048]{1,0:T(8,128)(2,1)}, bf16[8,2048]{1,0:T(8,128)(2,1)S(1)}, u32[]{:S(2)}, u32[]{:S(2)}) collective-permute-start(bf16[8,2048]{1,0:T(8,128)(2,1)} %get-tuple-element.645), channel_id=1, source_target_pairs={{0,32},{16,48},{32,64},{48,80},{64,96},{80,112},{96,128},{112,144}... | collective-permute-start | bytes 98312 | tf_op jit(solution)/shard_map/while/body/eval_jaxpr/ppermute | solution.py:13
  263.2 125.5 %reduce-scatter.5.cloned.1.call-start = ((), (), s32[]{:S(2)}) async-start(), calls=%async_computation.3 | async-start | bytes 557056 | tf_op jit(solution)/shard_map/while/body/eval_jaxpr/reduce_scatter | solution.py:119
  263.2 28.5 %collective-permute-start = (bf16[8,2048]{1,0:T(8,128)(2,1)}, bf16[8,2048]{1,0:T(8,128)(2,1)S(1)}, u32[]{:S(2)}, u32[]{:S(2)}) collective-permute-start(bf16[8,2048]{1,0:T(8,128)(2,1)} %get-tuple-element.645), channel_id=1, source_target_pairs={{0,32},{16,48},{32,64},{48,80},{64,96},{80,112},{96,128},{112,144}... | collective-permute-start | bytes 98312 | tf_op jit(solution)/shard_map/while/body/eval_jaxpr/ppermute | solution.py:13
  391.1 125.5 %reduce-scatter.5.cloned.1.call-start = ((), (), s32[]{:S(2)}) async-start(), calls=%async_computation.3 | async-start | bytes 557056 | tf_op jit(solution)/shard_map/while/body/eval_jaxpr/reduce_scatter | solution.py:119
  391.1 28.5 %collective-permute-start = (bf16[8,2048]{1,0:T(8,128)(2,1)}, bf16[8,2048]{1,0:T(8,128)(2,1)S(1)}, u32[]{:S(2)}, u32[]{:S(2)}) collective-permute-start(bf16[8,2048]{1,0:T(8,128)(2,1)} %get-tuple-element.645), channel_id=1, source_target_pairs={{0,32},{16,48},{32,64},{48,80},{64,96},{80,112},{96,128},{112,144}... | collective-permute-start | bytes 98312 | tf_op jit(solution)/shard_map/while/body/eval_jaxpr/ppermute | solution.py:13
  519.0 124.7 %reduce-scatter.5.cloned.1.call-start = ((), (), s32[]{:S(2)}) async-start(), calls=%async_computation.3 | async-start | bytes 557056 | tf_op jit(solution)/shard_map/while/body/eval_jaxpr/reduce_scatter | solution.py:119
  519.0 28.5 %collective-permute-start = (bf16[8,2048]{1,0:T(8,128)(2,1)}, bf16[8,2048]{1,0:T(8,128)(2,1)S(1)}, u32[]{:S(2)}, u32[]{:S(2)}) collective-permute-start(bf16[8,2048]{1,0:T(8,128)(2,1)} %get-tuple-element.645), channel_id=1, source_target_pairs={{0,32},{16,48},{32,64},{48,80},{64,96},{80,112},{96,128},{112,144}... | collective-permute-start | bytes 98312 | tf_op jit(solution)/shard_map/while/body/eval_jaxpr/ppermute | solution.py:13
  646.1 125.9 %reduce-scatter.5.cloned.1.call-start = ((), (), s32[]{:S(2)}) async-start(), calls=%async_computation.3 | async-start | bytes 557056 | tf_op jit(solution)/shard_map/while/body/eval_jaxpr/reduce_scatter | solution.py:119
  646.1 28.5 %collective-permute-start = (bf16[8,2048]{1,0:T(8,128)(2,1)}, bf16[8,2048]{1,0:T(8,128)(2,1)S(1)}, u32[]{:S(2)}, u32[]{:S(2)}) collective-permute-start(bf16[8,2048]{1,0:T(8,128)(2,1)} %get-tuple-element.645), channel_id=1, source_target_pairs={{0,32},{16,48},{32,64},{48,80},{64,96},{80,112},{96,128},{112,144}... | collective-permute-start | bytes 98312 | tf_op jit(solution)/shard_map/while/body/eval_jaxpr/ppermute | solution.py:13
  774.4 126.0 %reduce-scatter.5.cloned.1.call-start = ((), (), s32[]{:S(2)}) async-start(), calls=%async_computation.3 | async-start | bytes 557056 | tf_op jit(solution)/shard_map/while/body/eval_jaxpr/reduce_scatter | solution.py:119
  774.4 28.5 %collective-permute-start = (bf16[8,2048]{1,0:T(8,128)(2,1)}, bf16[8,2048]{1,0:T(8,128)(2,1)S(1)}, u32[]{:S(2)}, u32[]{:S(2)}) collective-permute-start(bf16[8,2048]{1,0:T(8,128)(2,1)} %get-tuple-element.645), channel_id=1, source_target_pairs={{0,32},{16,48},{32,64},{48,80},{64,96},{80,112},{96,128},{112,144}... | collective-permute-start | bytes 98312 | tf_op jit(solution)/shard_map/while/body/eval_jaxpr/ppermute | solution.py:13
  902.7 126.1 %reduce-scatter.5.cloned.1.call-start = ((), (), s32[]{:S(2)}) async-start(), calls=%async_computation.3 | async-start | bytes 557056 | tf_op jit(solution)/shard_map/while/body/eval_jaxpr/reduce_scatter | solution.py:119
  902.7 28.5 %collective-permute-start = (bf16[8,2048]{1,0:T(8,128)(2,1)}, bf16[8,2048]{1,0:T(8,128)(2,1)S(1)}, u32[]{:S(2)}, u32[]{:S(2)}) collective-permute-start(bf16[8,2048]{1,0:T(8,128)(2,1)} %get-tuple-element.645), channel_id=1, source_target_pairs={{0,32},{16,48},{32,64},{48,80},{64,96},{80,112},{96,128},{112,144}... | collective-permute-start | bytes 98312 | tf_op jit(solution)/shard_map/while/body/eval_jaxpr/ppermute | solution.py:13
  953.8 1.2 copy-start.10
  1031.2 123.4 %reduce-scatter.5.cloned.1.call-start = ((), (), s32[]{:S(2)}) async-start(), calls=%async_computation.3 | async-start | bytes 557056 | tf_op jit(solution)/shard_map/while/body/eval_jaxpr/reduce_scatter | solution.py:119
  1031.2 28.5 %collective-permute-start = (bf16[8,2048]{1,0:T(8,128)(2,1)}, bf16[8,2048]{1,0:T(8,128)(2,1)S(1)}, u32[]{:S(2)}, u32[]{:S(2)}) collective-permute-start(bf16[8,2048]{1,0:T(8,128)(2,1)} %get-tuple-element.645), channel_id=1, source_target_pairs={{0,32},{16,48},{32,64},{48,80},{64,96},{80,112},{96,128},{112,144}... | collective-permute-start | bytes 98312 | tf_op jit(solution)/shard_map/while/body/eval_jaxpr/ppermute | solution.py:13
  1082.3 1.2 copy-start.10
  1156.9 12.5 %copy-start.4 = (f32[1,1024,256]{2,1,0:T(8,128)S(1)}, f32[1,1024,256]{2,1,0:T(8,128)}, u32[]{:S(2)}) copy-start(f32[1,1024,256]{2,1,0:T(8,128)} %param.27) | copy-start | bytes 3145732
  1158.3 11.2 collective-permute-start.1
  1160.7 19.9 %collective-permute-start.2 = (bf16[1024,256]{1,0:T(8,128)(2,1)S(1)}, bf16[1024,256]{1,0:T(8,128)(2,1)S(1)}, u32[]{:S(2)}, u32[]{:S(2)}) collective-permute-start(bf16[1024,256]{1,0:T(8,128)(2,1)S(1)} %dynamic-slice_convert_fusion.1), channel_id=1, source_target_pairs={{0,16},{16,0},{32,48},{48,32},{64,80},{80,64},{96,112},{112,96},{1... | collective-permute-start | bytes 1572872 | tf_op jit(solution)/shard_map/ppermute | solution.py:23
  1162.5 18.2 %copy-start.5 = (f32[1,1024,256]{2,1,0:T(8,128)S(1)}, f32[1,1024,256]{2,1,0:T(8,128)}, u32[]{:S(2)}) copy-start(f32[1,1024,256]{2,1,0:T(8,128)} %param.28) | copy-start | bytes 3145732
  1162.5 29.4 %collective-permute-start.3 = (bf16[256,1024]{1,0:T(8,128)(2,1)S(1)}, bf16[256,1024]{1,0:T(8,128)(2,1)S(1)}, u32[]{:S(2)}, u32[]{:S(2)}) collective-permute-start(bf16[256,1024]{1,0:T(8,128)(2,1)S(1)} %dynamic-slice_convert_fusion), channel_id=1, source_target_pairs={{0,16},{16,0},{32,48},{48,32},{64,80},{80,64},{96,112},{112,96},{1... | collective-permute-start | bytes 1572872 | tf_op jit(solution)/shard_map/ppermute | solution.py:23
  1171.8 20.1 %copy-start.6 = (f32[1,256,1024]{2,1,0:T(8,128)S(1)}, f32[1,256,1024]{2,1,0:T(8,128)}, u32[]{:S(2)}) copy-start(f32[1,256,1024]{2,1,0:T(8,128)} %param.29) | copy-start | bytes 3145732
Sparse Core Ops, SparseCore 0:
  61.6 70.6 reduce-scatter.2
  187.6 73.2 reduce-scatter.4
  315.4 73.3 reduce-scatter.4
  443.3 73.3 reduce-scatter.4
  571.2 72.5 reduce-scatter.4
  698.3 73.7 reduce-scatter.4
  826.5 73.7 reduce-scatter.4
  957.5 71.2 reduce-scatter.4
  1085.9 68.5 reduce-scatter.4
where the time goes:
time: 1210 us; the launch traced here: 1200 us
  waiting for transfers between devices  644 us (53%)
  blocking collectives  435 us (36%)
  other arithmetic  37.8 us (3%)
  local copies, waits for them, and re-layouts  30.1 us (2%)
  matrix products  26 us (2%)
  between operations  13.9 us (1%)
  starting transfers between devices  13.1 us (1%)
    reduce_scatter x9, waiting for transfers between devices, process(): lax.psum_scatter(lax.cond(active, compute, quiet).astype(jnp.bfloat16), '...  620 us
    all_gather x9, blocking collectives, process(): full_rows = lax.all_gather(normed[slot], 'tp', axis=0, tiled=True)  238 us
    all_gather x9, blocking collectives, process(): incoming_rows = lax.all_gather(local_in, 'tp', axis=0, tiled=True)  198 us
  transfers between devices with their start and end apart: 20, of which 12 were waited for; matrix products, arithmetic and copies ran while one was open for 4% of the time, Pallas kernels for 0%

commit v1 on v0

v1 whole, which is shorter than its diff:
```python
import jax
import jax.numpy as jnp
from jax import lax
from jax.sharding import PartitionSpec as P

epsilon = 1e-05
momentum_decay = 0.9
bf16 = jnp.bfloat16
f32 = jnp.float32


def dot(left, right, dims):
    return lax.dot_general(left, right, ((dims[:1], dims[1:]), ((), ())), preferred_element_type=f32)


def shards(
    layer_inputs,
    cotangent,
    gate_weight,
    up_weight,
    down_weight,
    gate_momentum,
    up_momentum,
    down_momentum,
):
    segments = lax.axis_size("segment")
    tp = lax.axis_size("tp")
    depth = segments // 2
    segment = lax.axis_index("segment")
    direction = segment % 2
    position = segment // 2
    core = lax.axis_index("tp") % 2
    width = layer_inputs.shape[3]
    half = width // 2
    hidden_dev = gate_weight.shape[2]
    chips = [list(range(c, tp, 2)) for c in range(2)]
    other_core = [(i, i ^ 1) for i in range(tp)]
    pair = [(i, i ^ 1) for i in range(segments)]
    mirror = [
        ((s * tp + t), ((s ^ 1) * tp + (t ^ 1))) for s in range(segments) for t in range(tp)
    ]

    def swap(block):
        return lax.ppermute(block, "tp", other_core)

    def gathered(rows):
        copies = jnp.broadcast_to(rows[None], (tp // 2,) + rows.shape)
        out = lax.all_to_all(copies, "tp", 0, 0, axis_index_groups=chips, tiled=True)
        return out

    def scattered(parts):
        blocks = parts.reshape(tp // 2, -1, width)
        out = lax.all_to_all(blocks, "tp", 0, 0, axis_index_groups=chips, tiled=True)
        return jnp.sum(out.astype(f32), axis=0)

    entry = lax.dynamic_index_in_dim(cotangent, direction, 0, keepdims=False)
    stacked = jnp.stack([layer_inputs[0], entry], axis=1)
    mine = lax.dynamic_index_in_dim(stacked, core, 0, keepdims=False)
    theirs = lax.dynamic_index_in_dim(stacked, 1 - core, 0, keepdims=False)
    block = jnp.concatenate([mine, swap(theirs)], axis=1)
    inputs = block[0].astype(f32)
    rows_chip = inputs.shape[0]
    inverse_norm = lax.rsqrt(jnp.mean(inputs * inputs, axis=-1, keepdims=True) + epsilon)
    exact = inputs * inverse_norm
    normed = exact.astype(bf16)
    local_in = block[1]

    gate_w = jnp.concatenate([gate_weight[0], swap(gate_weight[0])], axis=1)
    up_w = jnp.concatenate([up_weight[0], swap(up_weight[0])], axis=1)
    down_w = jnp.concatenate([down_weight[0], swap(down_weight[0])], axis=0)

    first = gathered(jnp.concatenate([normed, local_in], axis=0))
    full_normed = first[:, :rows_chip].reshape(-1, width)
    full_in = first[:, rows_chip:].reshape(-1, width)

    gate = dot(full_normed, gate_w, (1, 0))
    up = dot(full_normed, up_w, (1, 0))
    sigma = jax.nn.sigmoid(gate)
    silu = gate * sigma
    hidden = (silu * up).astype(bf16)
    slope = up * sigma * (1.0 + gate * (1.0 - sigma))

    for tick in range(depth):
        if tick:
            route = [(2 * tick - 2 + d, 2 * tick + d) for d in range(2)]
            received = lax.ppermute(back, "segment", route)
            local_in = jnp.where(position == tick, received, local_in)
            full_in = gathered(local_in).reshape(-1, width)
        hidden_grad = dot(full_in, down_w, (1, 1))
        gate_grad = (hidden_grad * slope).astype(bf16)
        up_grad = (hidden_grad * silu).astype(bf16)
        parts = dot(gate_grad, gate_w, (1, 1)) + dot(up_grad, up_w, (1, 1))
        normed_grad = scattered(parts.astype(bf16))
        back = local_in.astype(f32) + inverse_norm * (
            normed_grad - exact * jnp.mean(normed_grad * exact, axis=-1, keepdims=True)
        )
        back = back.astype(bf16)

    rows_dev = rows_chip // 2
    mine_back, other_back = back[:rows_dev], swap(back[rows_dev:])
    low = core == 0
    input_gradient = jnp.stack(
        [jnp.where(low, mine_back, other_back), jnp.where(low, other_back, mine_back)]
    )

    keep = direction * half
    give = half - keep

    def features(rows, start):
        return lax.dynamic_slice_in_dim(rows, start, half, 1)

    def all_rows(rows):
        here = jnp.concatenate(
            [features(rows, keep), lax.ppermute(features(rows, give), "segment", pair)], axis=0
        )
        return jnp.concatenate([here, swap(here)], axis=0)

    def all_units(units):
        own, other = units[:, :hidden_dev], units[:, hidden_dev:]
        return jnp.concatenate(
            [
                own,
                lax.ppermute(own, "segment", pair),
                swap(other),
                lax.ppermute(other, ("segment", "tp"), mirror),
            ],
            axis=0,
        )

    def of(units, which):
        return lax.slice_in_dim(units, which * hidden_dev, (which + 1) * hidden_dev, axis=1)

    factors = [
        jnp.concatenate([of(hidden, w), of(gate_grad, w), of(up_grad, w)], axis=1) for w in range(2)
    ]
    units = jnp.concatenate(
        [
            factors[0],
            lax.ppermute(factors[0], "segment", pair),
            swap(factors[1]),
            lax.ppermute(factors[1], ("segment", "tp"), mirror),
        ],
        axis=0,
    )
    rows_normed = all_rows(full_normed)
    rows_in = all_rows(full_in)
    gate_share = dot(rows_normed, of(units, 1), (0, 0))
    up_share = dot(rows_normed, of(units, 2), (0, 0))
    down_share = dot(of(units, 0), rows_in, (0, 0))
    new_gate = (momentum_decay * gate_momentum[0] + gate_share)[None]
    new_up = (momentum_decay * up_momentum[0] + up_share)[None]
    new_down = (momentum_decay * down_momentum[0] + down_share)[None]
    return (input_gradient[None], new_gate, new_up, new_down)


def solution(mesh):
    return jax.shard_map(
        shards,
        mesh=mesh,
        in_specs=(
            P("segment", None, "tp", None),
            P(None, None, "tp", None),
            P("segment", None, "tp"),
            P("segment", None, "tp"),
            P("segment", "tp", None),
            P("segment", None, "tp"),
            P("segment", None, "tp"),
            P("segment", "tp", None),
        ),
        out_specs=(
            P("segment", None, "tp", None),
            P("segment", None, "tp"),
            P("segment", None, "tp"),
            P("segment", "tp", None),
        ),
        check_vma=False,
    )
```

time: 1210 us -> 330 us (0.27)
  waiting for transfers between devices: 644 us -> 49.2 us
  blocking collectives: 435 us -> 157 us
  starting transfers between devices: 13.1 us -> 52.8 us
  other arithmetic: 37.8 us -> 9.14 us
  matrix products: 26 us -> 50.5 us
  local copies, waits for them, and re-layouts: 30.1 us -> 7.55 us
  between operations: 13.9 us -> 1.55 us
    reduce_scatter x9 -> x0, waiting for transfers between devices: 620 us -> none  [process(): lax.psum_scatter(lax.cond(active, compute, quiet).astype(jnp.bfloat16), '...]
    all_gather x18 -> x0, blocking collectives: 435 us -> none  [the longest x9 238 us: process(): full_rows = lax.all_gather(normed[slot], 'tp', axis=0, tiled=True)]
    all_to_all x0 -> x13, blocking collectives: none -> 157 us  [the longest x7 83 us: scattered(): lax.all_to_all(blocks, 'tp', 0, 0, axis_index_groups=chips, tiled=True)]
    dot_general x16 -> x29, matrix products: 26 us -> 50.5 us  [dot(): lax.dot_general(left, right, ((dims[:1], dims[1:]), ((), ())), preferred_...]
    ppermute x11 -> x19, starting transfers between devices: 13.1 us -> 36.4 us  [the longest x8 29.1 us: swap(): return lax.ppermute(block, 'tp', other_core)]
    all_to_all x0 -> x3, waiting for transfers between devices: none -> 19.4 us  [the longest x2 15.4 us: gathered(): lax.all_to_all(copies, 'tp', 0, 0, axis_index_groups=chips, tiled=True)]
    all_to_all x0 -> x3, starting transfers between devices: none -> 16.4 us  [the longest x2 9.38 us: gathered(): lax.all_to_all(copies, 'tp', 0, 0, axis_index_groups=chips, tiled=True)]
    dynamic_update_slice x9 -> x0, other arithmetic: 13.2 us -> none  [process(): lax.dynamic_update_index_in_dim(backs, jnp.where(active, back, backs[slot...]
  transfers between devices with their start and end apart: 20 -> 22, of which waited for: 12 -> 7; matrix products, arithmetic and copies ran while one was open for 4% -> 7% of each run, Pallas kernels for 0% -> 0%
where the time goes in v1:
time: 330 us; the launch traced here: 328 us
  blocking collectives  157 us (48%)
  starting transfers between devices  52.8 us (16%)
  matrix products  50.5 us (15%)
  waiting for transfers between devices  49.2 us (15%)
  other arithmetic  9.14 us (3%)
  local copies, waits for them, and re-layouts  7.55 us (2%)
    all_to_all x7, blocking collectives, scattered(): lax.all_to_all(blocks, 'tp', 0, 0, axis_index_groups=chips, tiled=True)  83 us
    all_to_all x6, blocking collectives, gathered(): lax.all_to_all(copies, 'tp', 0, 0, axis_index_groups=chips, tiled=True)  74.5 us
    dot_general x29, matrix products, dot(): lax.dot_general(left, right, ((dims[:1], dims[1:]), ((), ())), preferred_...  50.5 us
    ppermute x8, starting transfers between devices, swap(): return lax.ppermute(block, 'tp', other_core)  29.1 us
    ppermute x7, waiting for transfers between devices, shards(): received = lax.ppermute(back, 'segment', route)  23.6 us
    all_to_all x2, waiting for transfers between devices, gathered(): lax.all_to_all(copies, 'tp', 0, 0, axis_index_groups=chips, tiled=True)  15.4 us
    all_to_all x2, starting transfers between devices, gathered(): lax.all_to_all(copies, 'tp', 0, 0, axis_index_groups=chips, tiled=True)  9.38 us
    all_to_all x1, starting transfers between devices, scattered(): lax.all_to_all(blocks, 'tp', 0, 0, axis_index_groups=chips, tiled=True)  6.98 us
  transfers between devices with their start and end apart: 22, of which 7 were waited for; matrix products, arithmetic and copies ran while one was open for 7% of the time, Pallas kernels for 0%

profile of v1, /device:TPU:227, one launch (start us, length us, event | category | flops | bytes accessed | tf_op | source)
XLA Modules:
  0.0 328.2 jit_solution(13260332763530598062)
XLA Ops:
  0.7 0.9 copy-done
  1.5 0.8 fusion.88
  2.3 0.8 collective-permute-start
  3.1 0.9 collective-permute-done
  4.3 1.1 broadcast_in_dim.24
  5.4 5.9 %all-to-all-start = ((bf16[8,32,2048]{2,1,0:T(8,128)(2,1)}), bf16[8,32,2048]{2,1,0:T(8,128)(2,1)S(1)}, u32[]{:S(2)}, u32[]{:S(2)}) async-start(bf16[8,32,2048]{2,1,0:T(8,128)(2,1)} %broadcast_in_dim.24), calls=%async_computation | async-start | bytes 2097152 | tf_op jit(solution)/shard_map/all_to_all | solution.py:48
  11.2 0.7 collective-permute-start.3
  12.5 15.4 %all-to-all-done = bf16[8,32,2048]{2,1,0:T(8,128)(2,1)S(1)} async-done(((bf16[8,32,2048]{2,1,0:T(8,128)(2,1)}), bf16[8,32,2048]{2,1,0:T(8,128)(2,1)S(1)}, u32[]{:S(2)}, u32[]{:S(2)}) %all-to-all-start) | async-done | bytes 1048608 | tf_op jit(solution)/shard_map/all_to_all | solution.py:48
  28.5 0.9 copy-done.13
  29.4 2.4 multiply_convert_fusion
  31.8 2.1 fusion.109
  33.9 2.0 fusion.78
  36.0 0.8 fusion
  36.8 13.9 %all_to_all.80 = bf16[8,16,2048]{2,1,0:T(8,128)(2,1)S(1)} all-to-all(bf16[8,16,2048]{2,1,0:T(8,128)(2,1)S(1)} %bitcast.78), channel_id=1, replica_groups={{0,2,4,6,8,10,12,14},{1,3,5,7,9,11,13,15},{16,18,20,22,24,26,28,30},{17..., dimensions={0} | all-to-all | bytes 1048576 | tf_op jit(solution)/shard_map/all_to_all | solution.py:53
  51.8 13.0 %all_to_all.81 = bf16[8,16,2048]{2,1,0:T(8,128)(2,1)S(1)} all-to-all(bf16[8,16,2048]{2,1,0:T(8,128)(2,1)S(1)} %broadcast_in_dim.25), channel_id=1, replica_groups={{0,2,4,6,8,10,12,14},{1,3,5,7,9,11,13,15},{16,18,20,22,24,26,28,30},{17..., dimensions={0} | all-to-all | bytes 1048576 | tf_op jit(solution)/shard_map/all_to_all | solution.py:48
  64.8 2.1 fusion.108
  67.0 2.0 fusion.79
  69.1 0.8 fusion.1
  69.9 11.5 %all_to_all.82 = bf16[8,16,2048]{2,1,0:T(8,128)(2,1)S(1)} all-to-all(bf16[8,16,2048]{2,1,0:T(8,128)(2,1)S(1)} %bitcast.79), channel_id=1, replica_groups={{0,2,4,6,8,10,12,14},{1,3,5,7,9,11,13,15},{16,18,20,22,24,26,28,30},{17..., dimensions={0} | all-to-all | bytes 1048576 | tf_op jit(solution)/shard_map/all_to_all | solution.py:53
  82.5 11.7 %all_to_all.83 = bf16[8,16,2048]{2,1,0:T(8,128)(2,1)S(1)} all-to-all(bf16[8,16,2048]{2,1,0:T(8,128)(2,1)S(1)} %broadcast_in_dim.26), channel_id=1, replica_groups={{0,2,4,6,8,10,12,14},{1,3,5,7,9,11,13,15},{16,18,20,22,24,26,28,30},{17..., dimensions={0} | all-to-all | bytes 1048576 | tf_op jit(solution)/shard_map/all_to_all | solution.py:48
  94.3 2.1 fusion.107
  96.4 2.0 fusion.80
  98.5 0.8 fusion.2
  99.3 11.5 %all_to_all.84 = bf16[8,16,2048]{2,1,0:T(8,128)(2,1)S(1)} all-to-all(bf16[8,16,2048]{2,1,0:T(8,128)(2,1)S(1)} %bitcast.80), channel_id=1, replica_groups={{0,2,4,6,8,10,12,14},{1,3,5,7,9,11,13,15},{16,18,20,22,24,26,28,30},{17..., dimensions={0} | all-to-all | bytes 1048576 | tf_op jit(solution)/shard_map/all_to_all | solution.py:53
  112.0 11.6 %all_to_all.85 = bf16[8,16,2048]{2,1,0:T(8,128)(2,1)S(1)} all-to-all(bf16[8,16,2048]{2,1,0:T(8,128)(2,1)S(1)} %broadcast_in_dim.27), channel_id=1, replica_groups={{0,2,4,6,8,10,12,14},{1,3,5,7,9,11,13,15},{16,18,20,22,24,26,28,30},{17..., dimensions={0} | all-to-all | bytes 1048576 | tf_op jit(solution)/shard_map/all_to_all | solution.py:48
  123.6 2.1 fusion.106
  125.7 2.0 fusion.81
  127.8 0.8 fusion.3
  128.6 11.5 %all_to_all.86 = bf16[8,16,2048]{2,1,0:T(8,128)(2,1)S(1)} all-to-all(bf16[8,16,2048]{2,1,0:T(8,128)(2,1)S(1)} %bitcast.81), channel_id=1, replica_groups={{0,2,4,6,8,10,12,14},{1,3,5,7,9,11,13,15},{16,18,20,22,24,26,28,30},{17..., dimensions={0} | all-to-all | bytes 1048576 | tf_op jit(solution)/shard_map/all_to_all | solution.py:53
  141.2 11.6 %all_to_all.87 = bf16[8,16,2048]{2,1,0:T(8,128)(2,1)S(1)} all-to-all(bf16[8,16,2048]{2,1,0:T(8,128)(2,1)S(1)} %broadcast_in_dim.28), channel_id=1, replica_groups={{0,2,4,6,8,10,12,14},{1,3,5,7,9,11,13,15},{16,18,20,22,24,26,28,30},{17..., dimensions={0} | all-to-all | bytes 1048576 | tf_op jit(solution)/shard_map/all_to_all | solution.py:48
  152.8 2.1 fusion.105
  155.0 2.0 fusion.82
  157.0 0.8 fusion.4
  157.9 11.5 %all_to_all.88 = bf16[8,16,2048]{2,1,0:T(8,128)(2,1)S(1)} all-to-all(bf16[8,16,2048]{2,1,0:T(8,128)(2,1)S(1)} %bitcast.82), channel_id=1, replica_groups={{0,2,4,6,8,10,12,14},{1,3,5,7,9,11,13,15},{16,18,20,22,24,26,28,30},{17..., dimensions={0} | all-to-all | bytes 1048576 | tf_op jit(solution)/shard_map/all_to_all | solution.py:53
  170.5 12.1 %all_to_all.89 = bf16[8,16,2048]{2,1,0:T(8,128)(2,1)S(1)} all-to-all(bf16[8,16,2048]{2,1,0:T(8,128)(2,1)S(1)} %broadcast_in_dim.29), channel_id=1, replica_groups={{0,2,4,6,8,10,12,14},{1,3,5,7,9,11,13,15},{16,18,20,22,24,26,28,30},{17..., dimensions={0} | all-to-all | bytes 1048576 | tf_op jit(solution)/shard_map/all_to_all | solution.py:48
  182.6 2.1 fusion.104
  184.7 2.0 fusion.83
  186.8 0.8 fusion.5
  187.6 11.5 %all_to_all.90 = bf16[8,16,2048]{2,1,0:T(8,128)(2,1)S(1)} all-to-all(bf16[8,16,2048]{2,1,0:T(8,128)(2,1)S(1)} %bitcast.83), channel_id=1, replica_groups={{0,2,4,6,8,10,12,14},{1,3,5,7,9,11,13,15},{16,18,20,22,24,26,28,30},{17..., dimensions={0} | all-to-all | bytes 1048576 | tf_op jit(solution)/shard_map/all_to_all | solution.py:53
  200.2 14.4 %all_to_all.91 = bf16[8,16,2048]{2,1,0:T(8,128)(2,1)S(1)} all-to-all(bf16[8,16,2048]{2,1,0:T(8,128)(2,1)S(1)} %broadcast_in_dim.30), channel_id=1, replica_groups={{0,2,4,6,8,10,12,14},{1,3,5,7,9,11,13,15},{16,18,20,22,24,26,28,30},{17..., dimensions={0} | all-to-all | bytes 1048576 | tf_op jit(solution)/shard_map/all_to_all | solution.py:48
  214.7 2.1 fusion.103
  216.8 2.0 fusion.84
  218.9 0.8 fusion.6
  219.7 11.7 %all_to_all.92 = bf16[8,16,2048]{2,1,0:T(8,128)(2,1)S(1)} all-to-all(bf16[8,16,2048]{2,1,0:T(8,128)(2,1)S(1)} %bitcast.84), channel_id=1, replica_groups={{0,2,4,6,8,10,12,14},{1,3,5,7,9,11,13,15},{16,18,20,22,24,26,28,30},{17..., dimensions={0} | all-to-all | bytes 1048576 | tf_op jit(solution)/shard_map/all_to_all | solution.py:53
  231.8 1.3 collective-permute-start.10
  233.1 23.6 %collective-permute-done.10 = bf16[16,2048]{1,0:T(8,128)(2,1)S(1)} collective-permute-done((bf16[16,2048]{1,0:T(8,128)(2,1)S(1)}, bf16[16,2048]{1,0:T(8,128)(2,1)S(1)}, u32[]{:S(2)}, u32[]{:S(2)}) %collective-permute-start.10) | collective-permute-done | bytes 65568 | tf_op jit(solution)/shard_map/ppermute | solution.py:86
  256.7 0.8 broadcast_in_dim.31
  257.6 3.5 %all-to-all-start.14 = ((bf16[8,16,2048]{2,1,0:T(8,128)(2,1)}), bf16[8,16,2048]{2,1,0:T(8,128)(2,1)S(1)}, u32[]{:S(2)}, u32[]{:S(2)}) async-start(bf16[8,16,2048]{2,1,0:T(8,128)(2,1)} %broadcast_in_dim.31), calls=%async_computation.14 | async-start | bytes 1048576 | tf_op jit(solution)/shard_map/all_to_all | solution.py:48
  261.1 1.8 constant_dynamic-slice_fusion.3
  262.8 1.5 fusion.115
  264.3 4.0 %collective-permute-done.12 = bf16[128,1024]{1,0:T(8,128)(2,1)} collective-permute-done((bf16[128,1024]{1,0:T(8,128)(2,1)}, bf16[128,1024]{1,0:T(8,128)(2,1)}, u32[]{:S(2)}, u32[]{:S(2)}) %collective-permute-start.12) | collective-permute-done | bytes 262176 | tf_op jit(solution)/shard_map/ppermute | solution.py:114
  268.4 1.8 pad_maximum_fusion.5
  270.1 25.1 %collective-permute-start.13 = (bf16[256,1024]{1,0:T(8,128)(2,1)}, bf16[256,1024]{1,0:T(8,128)(2,1)}, u32[]{:S(2)}, u32[]{:S(2)}) collective-permute-start(bf16[256,1024]{1,0:T(8,128)(2,1)} %pad_maximum_fusion.5), channel_id=1, source_target_pairs={{0,1},{1,0},{2,3},{3,2},{4,5},{5,4},{6,7},{7,6},{8,9},{9,8},{10,11... | collective-permute-start | bytes 1572872 | tf_op jit(solution)/shard_map/ppermute | solution.py:44
  295.2 2.5 multiply_convert_fusion.2
  299.2 1.7 collective-permute-start.14
  301.0 2.0 fusion.111
  303.0 1.6 fusion.7
  304.6 7.0 %all-to-all-start.15 = ((bf16[8,16,2048]{2,1,0:T(8,128)(2,1)}), bf16[8,16,2048]{2,1,0:T(8,128)(2,1)S(1)}, u32[]{:S(2)}, u32[]{:S(2)}) async-start(bf16[8,16,2048]{2,1,0:T(8,128)(2,1)} %bitcast.85), calls=%async_computation.15 | async-start | bytes 1048576 | tf_op jit(solution)/shard_map/all_to_all | solution.py:53
  312.0 1.2 pad_maximum_fusion.4
  313.2 2.6 fusion.10
  315.9 2.6 fusion.9
  318.4 4.0 %all-to-all-done.15 = bf16[8,16,2048]{2,1,0:T(8,128)(2,1)S(1)} async-done(((bf16[8,16,2048]{2,1,0:T(8,128)(2,1)}), bf16[8,16,2048]{2,1,0:T(8,128)(2,1)S(1)}, u32[]{:S(2)}, u32[]{:S(2)}) %all-to-all-start.15) | async-done | bytes 524320 | tf_op jit(solution)/shard_map/all_to_all | solution.py:53
  322.9 1.8 collective-permute-start.11
  326.7 1.4 fusion.8
  (139 shorter events, 12.7 us)
Async XLA Ops:
  0.6 0.9 copy-start
  2.3 1.7 collective-permute-start
  5.3 5.9 %copy-start.1 = (bf16[1,2048,256]{2,1,0:T(8,128)(2,1)S(1)}, bf16[1,2048,256]{2,1,0:T(8,128)(2,1)}, u32[]{:S(2)}) copy-start(bf16[1,2048,256]{2,1,0:T(8,128)(2,1)} %param.10) | copy-start | bytes 3145732
  5.4 22.5 %all-to-all-start = ((bf16[8,32,2048]{2,1,0:T(8,128)(2,1)}), bf16[8,32,2048]{2,1,0:T(8,128)(2,1)S(1)}, u32[]{:S(2)}, u32[]{:S(2)}) async-start(bf16[8,32,2048]{2,1,0:T(8,128)(2,1)} %broadcast_in_dim.24), calls=%async_computation | async-start | bytes 2097152 | tf_op jit(solution)/shard_map/all_to_all | solution.py:48
  11.2 16.8 %collective-permute-start.3 = (bf16[2048,256]{1,0:T(8,128)(2,1)S(1)}, bf16[2048,256]{1,0:T(8,128)(2,1)S(1)}, u32[]{:S(2)}, u32[]{:S(2)}) collective-permute-start(bf16[2048,256]{1,0:T(8,128)(2,1)S(1)} %bitcast.63), channel_id=1, source_target_pairs={{0,1},{1,0},{2,3},{3,2},{4,5},{5,4},{6,7},{7,6},{8,9},{9,8},{10,11... | collective-permute-start | bytes 3145736 | tf_op jit(solution)/shard_map/ppermute | solution.py:44
  12.0 16.5 %collective-permute-start.2 = (bf16[2048,256]{1,0:T(8,128)(2,1)}, bf16[2048,256]{1,0:T(8,128)(2,1)}, u32[]{:S(2)}, u32[]{:S(2)}) collective-permute-start(bf16[2048,256]{1,0:T(8,128)(2,1)} %bitcast.103), channel_id=1, source_target_pairs={{0,1},{1,0},{2,3},{3,2},{4,5},{5,4},{6,7},{7,6},{8,9},{9,8},{10,11... | collective-permute-start | bytes 3145736 | tf_op jit(solution)/shard_map/ppermute | solution.py:44
  12.1 19.8 %collective-permute-start.1 = (bf16[256,2048]{1,0:T(8,128)(2,1)}, bf16[256,2048]{1,0:T(8,128)(2,1)}, u32[]{:S(2)}, u32[]{:S(2)}) collective-permute-start(bf16[256,2048]{1,0:T(8,128)(2,1)} %bitcast.94), channel_id=1, source_target_pairs={{0,1},{1,0},{2,3},{3,2},{4,5},{5,4},{6,7},{7,6},{8,9},{9,8},{10,11... | collective-permute-start | bytes 3145736 | tf_op jit(solution)/shard_map/ppermute | solution.py:44
  28.0 3.9 %copy-start.2 = (bf16[8,16,2048]{2,1,0:T(8,128)(2,1)}, bf16[8,16,2048]{2,1,0:T(8,128)(2,1)S(1)}, u32[]{:S(2)}) copy-start(bf16[8,16,2048]{2,1,0:T(8,128)(2,1)S(1)} %get-tuple-element.6) | copy-start | bytes 1572868
  28.0 1.4 copy-start.13
  28.5 188.3 %copy-start.24 = (f32[128,512]{1,0:T(8,128)}, f32[128,512]{1,0:T(8,128)S(1)}, u32[]{:S(2)}) copy-start(f32[128,512]{1,0:T(8,128)S(1)} %fusion.110) | copy-start | bytes 786436
  28.5 3.3 %copy-start.6 = (bf16[1,256,2048]{2,1,0:T(8,128)(2,1)S(1)}, bf16[1,256,2048]{2,1,0:T(8,128)(2,1)}, u32[]{:S(2)}) copy-start(bf16[1,256,2048]{2,1,0:T(8,128)(2,1)} %param.12) | copy-start | bytes 3145732
  51.0 0.7 collective-permute-start.4
  51.7 13.1 %copy-start.7 = (bf16[1,256,2048]{2,1,0:T(8,128)(2,1)S(1)}, bf16[1,256,2048]{2,1,0:T(8,128)(2,1)}, u32[]{:S(2)}) copy-start(bf16[1,256,2048]{2,1,0:T(8,128)(2,1)} %param.12) | copy-start | bytes 3145732
  64.8 2.2 copy-start.14
  81.8 0.7 collective-permute-start.5
  82.4 11.8 %copy-start.8 = (bf16[1,256,2048]{2,1,0:T(8,128)(2,1)S(1)}, bf16[1,256,2048]{2,1,0:T(8,128)(2,1)}, u32[]{:S(2)}) copy-start(bf16[1,256,2048]{2,1,0:T(8,128)(2,1)} %param.12) | copy-start | bytes 3145732
  94.3 2.2 copy-start.15
  111.2 0.7 collective-permute-start.6
  111.9 11.7 %copy-start.9 = (bf16[1,256,2048]{2,1,0:T(8,128)(2,1)S(1)}, bf16[1,256,2048]{2,1,0:T(8,128)(2,1)}, u32[]{:S(2)}) copy-start(bf16[1,256,2048]{2,1,0:T(8,128)(2,1)} %param.12) | copy-start | bytes 3145732
  123.6 2.2 copy-start.16
  140.5 0.7 collective-permute-start.7
  141.1 11.7 %copy-start.10 = (bf16[1,256,2048]{2,1,0:T(8,128)(2,1)S(1)}, bf16[1,256,2048]{2,1,0:T(8,128)(2,1)}, u32[]{:S(2)}) copy-start(bf16[1,256,2048]{2,1,0:T(8,128)(2,1)} %param.12) | copy-start | bytes 3145732
  152.8 2.2 copy-start.17
  169.7 0.7 collective-permute-start.8
  170.4 12.2 %copy-start.11 = (bf16[1,256,2048]{2,1,0:T(8,128)(2,1)S(1)}, bf16[1,256,2048]{2,1,0:T(8,128)(2,1)}, u32[]{:S(2)}) copy-start(bf16[1,256,2048]{2,1,0:T(8,128)(2,1)} %param.12) | copy-start | bytes 3145732
  182.6 2.2 copy-start.18
  199.5 0.7 collective-permute-start.9
  200.1 14.5 %copy-start.12 = (bf16[1,256,2048]{2,1,0:T(8,128)(2,1)S(1)}, bf16[1,256,2048]{2,1,0:T(8,128)(2,1)}, u32[]{:S(2)}) copy-start(bf16[1,256,2048]{2,1,0:T(8,128)(2,1)} %param.12) | copy-start | bytes 3145732
  214.6 2.2 copy-start.19
  231.8 24.9 %collective-permute-start.10 = (bf16[16,2048]{1,0:T(8,128)(2,1)S(1)}, bf16[16,2048]{1,0:T(8,128)(2,1)S(1)}, u32[]{:S(2)}, u32[]{:S(2)}) collective-permute-start(bf16[16,2048]{1,0:T(8,128)(2,1)S(1)} %fusion.71), channel_id=1, source_target_pairs={{192,224},{208,240},{193,225},{209,241},{194,226},{210,242},{195,2... | collective-permute-start | bytes 196616 | tf_op jit(solution)/shard_map/ppermute | solution.py:86
  257.6 37.7 %all-to-all-start.14 = ((bf16[8,16,2048]{2,1,0:T(8,128)(2,1)}), bf16[8,16,2048]{2,1,0:T(8,128)(2,1)S(1)}, u32[]{:S(2)}, u32[]{:S(2)}) async-start(bf16[8,16,2048]{2,1,0:T(8,128)(2,1)} %broadcast_in_dim.31), calls=%async_computation.14 | async-start | bytes 1048576 | tf_op jit(solution)/shard_map/all_to_all | solution.py:48
  262.8 5.5 %collective-permute-start.12 = (bf16[128,1024]{1,0:T(8,128)(2,1)}, bf16[128,1024]{1,0:T(8,128)(2,1)}, u32[]{:S(2)}, u32[]{:S(2)}) collective-permute-start(bf16[128,1024]{1,0:T(8,128)(2,1)} %get-tuple-element.13), channel_id=1, source_target_pairs={{0,16},{16,0},{32,48},{48,32},{64,80},{80,64},{96,112},{112,96},{1... | collective-permute-start | bytes 786440 | tf_op jit(solution)/shard_map/ppermute | solution.py:114
  270.1 43.1 %collective-permute-start.13 = (bf16[256,1024]{1,0:T(8,128)(2,1)}, bf16[256,1024]{1,0:T(8,128)(2,1)}, u32[]{:S(2)}, u32[]{:S(2)}) collective-permute-start(bf16[256,1024]{1,0:T(8,128)(2,1)} %pad_maximum_fusion.5), channel_id=1, source_target_pairs={{0,1},{1,0},{2,3},{3,2},{4,5},{5,4},{6,7},{7,6},{8,9},{9,8},{10,11... | collective-permute-start | bytes 1572872 | tf_op jit(solution)/shard_map/ppermute | solution.py:44
  295.2 2.5 copy-start.5
  297.7 3.3 %copy-start.20 = (bf16[1,2048,256]{2,1,0:T(8,128)(2,1)S(1)}, bf16[1,2048,256]{2,1,0:T(8,128)(2,1)}, u32[]{:S(2)}) copy-start(bf16[1,2048,256]{2,1,0:T(8,128)(2,1)} %param.11) | copy-start | bytes 3145732
  297.7 5.3 %copy-start.3 = (bf16[128,256]{1,0:T(8,128)(2,1)}, bf16[128,256]{1,0:T(8,128)(2,1)S(1)}, u32[]{:S(2)}) copy-start(bf16[128,256]{1,0:T(8,128)(2,1)S(1)} %get-tuple-element.27) | copy-start | bytes 196612
  298.4 13.6 %collective-permute-start.16 = (bf16[128,768]{1,0:T(8,128)(2,1)}, bf16[128,768]{1,0:T(8,128)(2,1)}, u32[]{:S(2)}, u32[]{:S(2)}) collective-permute-start(bf16[128,768]{1,0:T(8,128)(2,1)} %pad_maximum_fusion.10), channel_id=1, source_target_pairs={{0,17},{1,16},{2,19},{3,18},{4,21},{5,20},{6,23},{7,22},{8,25},{9,... | collective-permute-start | bytes 589832 | tf_op jit(solution)/shard_map/ppermute | solution.py:141
  298.5 13.6 %collective-permute-start.15 = (bf16[128,768]{1,0:T(8,128)(2,1)}, bf16[128,768]{1,0:T(8,128)(2,1)}, u32[]{:S(2)}, u32[]{:S(2)}) collective-permute-start(bf16[128,768]{1,0:T(8,128)(2,1)} %pad_maximum_fusion.10), channel_id=1, source_target_pairs={{0,1},{1,0},{2,3},{3,2},{4,5},{5,4},{6,7},{7,6},{8,9},{9,8},{10,11... | collective-permute-start | bytes 589832 | tf_op jit(solution)/shard_map/ppermute | solution.py:44
  299.2 12.8 %collective-permute-start.14 = (bf16[128,768]{1,0:T(8,128)(2,1)}, bf16[128,768]{1,0:T(8,128)(2,1)}, u32[]{:S(2)}, u32[]{:S(2)}) collective-permute-start(bf16[128,768]{1,0:T(8,128)(2,1)} %pad_maximum_fusion.9), channel_id=1, source_target_pairs={{0,16},{16,0},{32,48},{48,32},{64,80},{80,64},{96,112},{112,96},{1... | collective-permute-start | bytes 589832 | tf_op jit(solution)/shard_map/ppermute | solution.py:139
  304.6 7.4 %copy-start.4 = (bf16[128,256]{1,0:T(8,128)(2,1)S(1)}, bf16[128,256]{1,0:T(8,128)(2,1)}, u32[]{:S(2)}) copy-start(bf16[128,256]{1,0:T(8,128)(2,1)} %copy-done.3) | copy-start | bytes 196612
  304.6 17.8 %all-to-all-start.15 = ((bf16[8,16,2048]{2,1,0:T(8,128)(2,1)}), bf16[8,16,2048]{2,1,0:T(8,128)(2,1)S(1)}, u32[]{:S(2)}, u32[]{:S(2)}) async-start(bf16[8,16,2048]{2,1,0:T(8,128)(2,1)} %bitcast.85), calls=%async_computation.15 | async-start | bytes 1048576 | tf_op jit(solution)/shard_map/all_to_all | solution.py:53
  311.7 1.6 copy-start.21
  311.7 13.0 %collective-permute-start.17 = (bf16[128,1024]{1,0:T(8,128)(2,1)S(1)}, bf16[128,1024]{1,0:T(8,128)(2,1)S(1)}, u32[]{:S(2)}, u32[]{:S(2)}) collective-permute-start(bf16[128,1024]{1,0:T(8,128)(2,1)S(1)} %get-tuple-element.9), channel_id=1, source_target_pairs={{0,16},{16,0},{32,48},{48,32},{64,80},{80,64},{96,112},{112,96},{1... | collective-permute-start | bytes 786440 | tf_op jit(solution)/shard_map/ppermute | solution.py:114
  313.2 2.7 copy-start.22
  322.5 4.2 %copy-start.23 = (f32[1,256,1024]{2,1,0:T(8,128)S(1)}, f32[1,256,1024]{2,1,0:T(8,128)}, u32[]{:S(2)}) copy-start(f32[1,256,1024]{2,1,0:T(8,128)} %param.15) | copy-start | bytes 3145732
  322.9 2.6 collective-permute-start.11
  324.7 2.0 collective-permute-start.18
